TPU v7x, 32 devices: a whole 2x2x4 slice. The times are simulated.
32 devices in a mesh: section: 2 (over core), head: 4 (over z), blk: 4 (over y, x).
Axes of the slice: x: 2, y: 2, z: 4, core: 2. Of those that a mesh axis runs over, the one named last changes fastest.
Arguments:
- section_input: bfloat16 [2, 8, 256, 1536], P('section', 'blk')
- modulation: bfloat16 [2, 8, 2, 1536], P('section', 'blk'), may hold values from -3 to 3
- attn_gate: bfloat16 [2, 8, 1536], P('section', 'blk'), may hold values from -12 to 12
- qkv_weight: bfloat16 [2, 1536, 3, 1536], P('section', None, None, 'head'), may hold values from -0.15625 to 0.15625
- out_weight: bfloat16 [2, 1536, 1536], P('section', 'head'), may hold values from -0.15625 to 0.15625
- kv_cache: bfloat16 [2, 8, 256, 4, 2, 1536], P('section', None, 'blk', None, None, 'head'), may hold values from -9 to 9
- text_kv: bfloat16 [2, 8, 154, 2, 1536], P('section', 'blk', None, None, 'head')
- text_len: int32 [8], P('blk'), may hold values from 4 to 154, as said below
- patch_order: int32 [4, 4], replicated, may hold values from 0 to 3, each once within a row
- final_mod: bfloat16 [8, 2, 1536], P('blk'), may hold values from -3 to 3
- final_weight: bfloat16 [1536, 64], replicated, may hold values from -0.15625 to 0.15625
- latent: float32 [4, 128, 128], P('blk', 'section'), may hold values from -6 to 6
Outputs:
- section_output: bfloat16 [2, 8, 256, 1536], P('section', 'blk', None, 'head')
- cache_patch: bfloat16 [2, 8, 256, 2, 1536], P('section', None, 'blk', None, 'head')
- latent_next: float32 [4, 128, 128], P('blk', 'section')
Inputs may be any that keep to these rules, and one draw needn't show every extreme that they name: `text_len`: sequence 0 uses all 154 text positions. `patch_order`: each row is a permutation of the 4 patches.
All inputs are finite; a program needn't handle non-finite values.
Results may differ from a plain program's by a relative error of at most 0.0092.
Values may be sent and summed in bfloat16 or wider, within the bound.
A program may use at most 128 MiB of HBM per device.

v0:
```python
import jax
import jax.numpy as jnp
from jax import lax
from jax.sharding import PartitionSpec as P

HEAD_DIM = 64
norm_eps = 1e-06
guidance = 4.0
euler_step = -0.25


def passed_along(shard, axis, by):
    devices = lax.axis_size(axis)
    return lax.ppermute(shard, axis, [(i, (i + by) % devices) for i in range(devices)])


def layer_norm(values):
    row_mean = jnp.mean(values, axis=-1, keepdims=True)
    centered = values - row_mean
    row_var = jnp.mean(centered * centered, axis=-1, keepdims=True)
    return centered / jnp.sqrt(row_var + norm_eps)


def piece_scores(query_heads, key_piece, counted_piece):
    seq_dev = key_piece.shape[0]
    head_count = query_heads.shape[2]
    key_heads = key_piece.reshape(seq_dev, -1, head_count, HEAD_DIM)
    scores = jnp.einsum(
        "sqhd,skhd->shqk", query_heads, key_heads, preferred_element_type=jnp.float32
    ) * HEAD_DIM ** (-0.5)
    if counted_piece is not None:
        scores = jnp.where(counted_piece[:, None, None, :], scores, -1e30)
    return scores


def piece_values(probs_piece, value_piece, head_count):
    seq_dev = value_piece.shape[0]
    value_heads = value_piece.reshape(seq_dev, -1, head_count, HEAD_DIM)
    return jnp.einsum(
        "shqk,skhd->sqhd", probs_piece, value_heads, preferred_element_type=jnp.float32
    )


def shards(
    section_input,
    modulation,
    attn_gate,
    qkv_weight,
    out_weight,
    kv_cache,
    text_kv,
    text_len,
    patch_order,
    final_mod,
    final_weight,
    latent,
):
    section_index = lax.axis_index("section")
    seq_patch = jnp.repeat(
        lax.dynamic_index_in_dim(patch_order, section_index, 1, keepdims=False), 2
    )
    hidden_in = section_input[0]
    seq_dev, patch_rows, model_width = hidden_in.shape
    own_patch = lax.dynamic_slice_in_dim(seq_patch, lax.axis_index("blk") * seq_dev, seq_dev, 0)
    hidden_wide = hidden_in.astype(jnp.float32)
    shift_scale = modulation[0].astype(jnp.float32)
    normed = (layer_norm(hidden_wide) * (1.0 + shift_scale[:, 1:2]) + shift_scale[:, 0:1]).astype(
        jnp.bfloat16
    )
    group_width = qkv_weight.shape[3]
    projected = jnp.dot(
        normed.reshape(seq_dev * patch_rows, model_width),
        qkv_weight[0].reshape(model_width, 3 * group_width),
        preferred_element_type=jnp.float32,
    ).astype(jnp.bfloat16)
    projected = projected.reshape(seq_dev, patch_rows, 3, group_width)
    queries = projected[:, :, 0]
    key_new = projected[:, :, 1]
    value_new = projected[:, :, 2]
    fresh_kv = jnp.stack([key_new, value_new], axis=2)
    refreshed = lax.all_to_all(fresh_kv, "blk", split_axis=1, concat_axis=0, tiled=True)
    local_cache = kv_cache[0]
    patch_count = local_cache.shape[2]
    fetched = lax.all_to_all(local_cache, "blk", split_axis=0, concat_axis=1, tiled=True)
    keep_patch = jnp.arange(patch_count, dtype=jnp.int32)[None, :] != own_patch[:, None]
    stale_counted = jnp.tile(keep_patch, (1, patch_rows))
    stale_keys = fetched[:, :, :, 0].reshape(seq_dev, -1, group_width)
    stale_values = fetched[:, :, :, 1].reshape(seq_dev, -1, group_width)
    text_local = text_kv[0]
    text_count = text_local.shape[1]
    text_counted = jnp.arange(text_count, dtype=jnp.int32)[None, :] < text_len[:, None]
    head_count = group_width // HEAD_DIM
    query_heads = queries.reshape(seq_dev, patch_rows, head_count, HEAD_DIM)
    text_scores = piece_scores(query_heads, text_local[:, :, 0], text_counted)
    fresh_scores = piece_scores(query_heads, key_new, None)
    stale_scores = piece_scores(query_heads, stale_keys, stale_counted)
    row_max = jnp.maximum(
        jnp.maximum(
            jnp.max(text_scores, axis=-1, keepdims=True),
            jnp.max(fresh_scores, axis=-1, keepdims=True),
        ),
        jnp.max(stale_scores, axis=-1, keepdims=True),
    )
    text_weights = jnp.exp(text_scores - row_max)
    fresh_weights = jnp.exp(fresh_scores - row_max)
    stale_weights = jnp.exp(stale_scores - row_max)
    total = (
        jnp.sum(text_weights, axis=-1, keepdims=True)
        + jnp.sum(fresh_weights, axis=-1, keepdims=True)
        + jnp.sum(stale_weights, axis=-1, keepdims=True)
    )
    text_probs = (text_weights / total).astype(jnp.bfloat16)
    fresh_probs = (fresh_weights / total).astype(jnp.bfloat16)
    stale_probs = (stale_weights / total).astype(jnp.bfloat16)
    attended_wide = (
        piece_values(text_probs, text_local[:, :, 1], head_count)
        + piece_values(fresh_probs, value_new, head_count)
        + piece_values(stale_probs, stale_values, head_count)
    )
    attended = attended_wide.astype(jnp.bfloat16)
    partial_value = jnp.dot(
        attended.reshape(seq_dev * patch_rows, group_width),
        out_weight[0],
        preferred_element_type=jnp.float32,
    )
    gate_wide = attn_gate[0].astype(jnp.float32)[:, None, :]
    share_width = model_width // lax.axis_size("head")
    share_start = lax.axis_index("head") * share_width
    half_rows = patch_rows // 2
    share_sum = lax.psum_scatter(
        partial_value.reshape(seq_dev, patch_rows, model_width).astype(jnp.bfloat16),
        "head",
        scatter_dimension=2,
        tiled=True,
    ).astype(jnp.float32)
    own_hidden = lax.dynamic_slice_in_dim(hidden_wide, share_start, share_width, 2)
    own_gate = lax.dynamic_slice_in_dim(gate_wide, share_start, share_width, 2)
    layer_out = (own_hidden + own_gate * share_sum).astype(jnp.bfloat16)
    received = passed_along(layer_out, "section", 1)
    last_layer = jnp.where(section_index == 0, received, layer_out)
    last_half = lax.dynamic_slice_in_dim(last_layer, section_index * half_rows, half_rows, 1)
    final_rows = lax.all_gather(last_half, "head", axis=2, tiled=True)
    final_shift = final_mod.astype(jnp.float32)
    final_normed = (
        layer_norm(final_rows.astype(jnp.float32)) * (1.0 + final_shift[:, 1:2])
        + final_shift[:, 0:1]
    ).astype(jnp.bfloat16)
    velocity = jnp.dot(
        final_normed.reshape(seq_dev * half_rows, model_width),
        final_weight,
        preferred_element_type=jnp.float32,
    )
    velocity = velocity.reshape(seq_dev // 2, 2, -1)
    guided = velocity[:, 1] + guidance * (velocity[:, 0] - velocity[:, 1])
    latent_next = latent + euler_step * guided.reshape(latent.shape)
    return (received[None], refreshed[None], latent_next)


def solution(mesh):
    placed = (
        P("section", "blk", None, None),
        P("section", "blk", None, None),
        P("section", "blk", None),
        P("section", None, None, "head"),
        P("section", "head", None),
        P("section", None, "blk", None, None, "head"),
        P("section", "blk", None, None, "head"),
        P("blk"),
        P(),
        P("blk", None, None),
        P(),
        P("blk", "section", None),
    )
    return jax.shard_map(
        shards,
        mesh=mesh,
        in_specs=placed,
        out_specs=(
            P("section", "blk", None, "head"),
            P("section", None, "blk", None, "head"),
            P("blk", "section", None),
        ),
        check_vma=False,
    )
```

profile of v0, /device:TPU:0, one launch (start us, length us, event | category | flops | bytes accessed | tf_op | source)
XLA Modules:
  0.0 174.6 jit_solution(1458555649823151610)
XLA Ops:
  7.2 5.4 %all-to-all-start = ((bf16[8,64,4,2,384]{4,3,2,1,0:T(2,128)(2,1)}), bf16[8,64,4,2,384]{4,3,2,1,0:T(2,128)(2,1)}, u32[]{:S(2)}, u32[]{:S(2)}) async-start(bf16[8,64,4,2,384]{4,3,2,1,0:T(2,128)(2,1)} %bitcast.90), calls=%async_computation | async-start | bytes 6291456 | tf_op jit(solution)/shard_map/all_to_all | solution.py:84
  14.3 6.1 %copy.85 = bf16[1,1536,3,384]{1,3,2,0:T(8,128)(2,1)} copy(bf16[1,1536,3,384]{3,1,2,0:T(8,128)(2,1)} %param.15) | data formatting | bytes 7077888 | tf_op args[3]
  21.1 5.2 %convolution_convert_fusion = bf16[512,1152]{1,0:T(8,128)(2,1)} fusion(bf16[512,1536]{1,0:T(8,128)(2,1)S(1)} %bitcast.95, bf16[1536,1152]{0,1:T(8,128)(2,1)} %bitcast.89), kind=kOutput, calls=%fused_computation.14 | convolution fusion | flops 1812529152 | bytes 6291456 | tf_op jit(solution)/shard_map/dot_general | solution.py:71
  26.3 2.4 %copy.86 = bf16[512,1152]{0,1:T(8,128)(2,1)} copy(bf16[512,1152]{1,0:T(8,128)(2,1)} %convolution_convert_fusion) | data formatting | bytes 2359296 | tf_op jit(solution)/shard_map/convert_element_type | solution.py:75
  28.7 3.7 %reshape.237 = bf16[2,256,3,384]{1,0,3,2:T(2,128)(2,1)} reshape(bf16[512,1152]{0,1:T(8,128)(2,1)} %copy.86) | data formatting | bytes 2359296 | tf_op jit(solution)/shard_map/reshape | solution.py:76
  32.4 2.1 %fusion.35 = (bf16[2,256,1,384]{1,0,3,2:T(2,128)(2,1)S(1)}, bf16[2,256,1,384]{1,0,3,2:T(2,128)(2,1)S(1)}, bf16[2,256,1,384]{1,0,3,2:T(2,128)(2,1)S(1)}) fusion(bf16[2,256,3,384]{1,0,3,2:T(2,128)(2,1)} %reshape.237), kind=kLoop, calls=%fused_computation.71 | loop fusion | bytes 2359296 | tf_op jit(solution)/shard_map/slice | solution.py:79
  41.9 3.5 %fusion.9 = (f32[2,6,256]{2,1,0:T(8,128)}, f32[2,6,256,154]{2,3,1,0:T(8,128)}) fusion(pred[2,154]{1,0:T(4,128)(4,1)S(1)} %iota_compare_fusion, bf16[2,256,6,64]{1,3,2,0:T(8,128)(2,1)S(1)} %bitcast.86, bf16[2,154,6,64]{1,3,2,0:T(8,128)(2,1)} %bitcast.96), kind=kOutput, calls=%fused_computation.26 | convolution fusion | flops 61971456 | bytes 2534708 | tf_op jit(solution)/shard_map/sqhd,skhd->shqk/dot_general | solution.py:28
  45.3 2.9 %multiply_reduce_fusion.1 = (f32[2,6,256]{2,1,0:T(8,128)}, f32[2,6,256,256]{2,3,1,0:T(8,128)}) fusion(bf16[2,256,6,64]{1,3,2,0:T(8,128)(2,1)S(1)} %bitcast.87, bf16[2,256,6,64]{1,3,2,0:T(8,128)(2,1)S(1)} %bitcast.98), kind=kOutput, calls=%fused_computation.16 | convolution fusion | flops 102233088 | bytes 3944448 | tf_op jit(solution)/shard_map/sqhd,skhd->shqk/dot_general | solution.py:28
  49.8 3.4 %copy.90 = bf16[2,4,64,4,2,384]{5,3,2,1,0,4:T(4,128)(2,1)S(1)} copy(bf16[2,4,64,4,2,384]{5,4,3,2,0,1:T(2,128)(2,1)} %bitcast.13) | data formatting | bytes 6291456 | tf_op jit(solution)/shard_map/all_to_all | solution.py:84
  53.2 2.8 %fusion.34 = (bf16[2,256,4,1,384]{4,2,1,0,3:T(4,128)(2,1)}, bf16[2,256,4,1,384]{4,2,1,0,3:T(4,128)(2,1)}) fusion(bf16[2,256,4,2,384]{4,2,1,0,3:T(4,128)(2,1)S(1)} %bitcast.83), kind=kLoop, calls=%fused_computation.70 | loop fusion | bytes 6291456 | tf_op jit(solution)/shard_map/slice | solution.py:87
  56.0 6.0 %reshape_reshape_squeeze.6 = bf16[2,1024,6,64]{3,2,1,0:T(8,128)(2,1)} reshape(bf16[2,256,4,1,384]{4,2,1,0,3:T(4,128)(2,1)} %get-tuple-element.12) | data formatting | bytes 3145728 | tf_op jit(solution)/shard_map/reshape;reshape;squeeze | solution.py:27
  62.0 4.4 %fusion = (f32[2,6,256]{2,1,0:T(8,128)S(1)}, f32[2,6,256,1024]{3,2,1,0:T(8,128)S(1)}) fusion(pred[2,1024]{1,0:T(4,128)(4,1)S(1)} %tile.9, bf16[2,256,6,64]{1,3,2,0:T(8,128)(2,1)S(1)} %bitcast.88, bf16[2,1024,6,64]{3,2,1,0:T(8,128)(2,1)} %reshape_reshape_squeeze.6), kind=kOutput, calls=%fused_computation.3 | convolution fusion | flops 412087296 | bytes 14563328 | tf_op jit(solution)/shard_map/sqhd,skhd->shqk/dot_general | solution.py:28
  66.5 3.3 %fusion.1 = f32[2,6,256]{2,1,0:T(8,128)S(1)} fusion(f32[2,6,256,1024]{3,2,1,0:T(8,128)S(1)} %get-tuple-element.24, f32[2,6,256]{2,1,0:T(8,128)S(1)} %maximum_maximum_fusion, pred[2,1024]{1,0:T(4,128)(4,1)S(1)} %tile.9), kind=kLoop, calls=%fused_computation.4 | loop fusion | flops 12579840 | bytes 12609536 | tf_op jit(solution)/shard_map/reduce_sum | solution.py:110
  73.9 6.1 %reshape_reshape_squeeze.7 = bf16[2,1024,6,64]{3,2,1,0:T(8,128)(2,1)} reshape(bf16[2,256,4,1,384]{4,2,1,0,3:T(4,128)(2,1)} %get-tuple-element.13) | data formatting | bytes 3145728 | tf_op jit(solution)/shard_map/reshape;reshape;squeeze | solution.py:38
  80.0 2.8 %fusion.16 = f32[2,256,6,64]{1,3,2,0:T(8,128)S(1)} fusion(bf16[2,256,6,64]{1,3,2,0:T(8,128)(2,1)S(1)} %bitcast.101, f32[2,6,256,256]{2,3,1,0:T(8,128)} %get-tuple-element.28, f32[2,6,256]{2,1,0:T(8,128)S(1)} %add_add_fusion, f32[2,6,256]{2,1,0:T(8,128)S(1)} %maximum_maximum_fusion), kind=kOutput, calls=%fused_computation.33 | convolution fusion | flops 103809024 | bytes 4349952 | tf_op jit(solution)/shard_map/shqk,skhd->sqhd/dot_general | solution.py:39
  82.8 2.7 %copy-done.2 = f32[2,6,256,1024]{3,2,1,0:T(8,128)S(1)} copy-done((f32[2,6,256,1024]{3,2,1,0:T(8,128)S(1)}, f32[2,6,256,1024]{3,2,1,0:T(8,128)}, u32[]{:S(2)}) %copy-start.2) | copy-done | bytes 12582936
  85.5 5.7 %fusion.19 = f32[2,256,6,64]{1,3,2,0:T(8,128)S(1)} fusion(bf16[2,1024,6,64]{3,2,1,0:T(8,128)(2,1)} %reshape_reshape_squeeze.7, f32[2,6,256,1024]{3,2,1,0:T(8,128)S(1)} %copy-done.2, f32[2,6,256]{2,1,0:T(8,128)S(1)} %add_add_fusion, f32[2,6,256]{2,1,0:T(8,128)S(1)} %maximum_maximum_fusion, pred[2,1024]{1,0:T(4,128)(4,1)S(1)} %tile.9), kind=kOutput, calls=%fused_computation.37 | convolution fusion | flops 418381824 | bytes 14968832 | tf_op jit(solution)/shard_map/shqk,skhd->sqhd/dot_general | solution.py:39
  91.9 2.2 %convolution_convert_fusion.1 = bf16[2,256,1536]{2,1,0:T(8,128)(2,1)} fusion(bf16[2,256,384]{1,2,0:T(8,128)(2,1)S(1)} %bitcast.99, bf16[1,384,1536]{2,1,0:T(8,128)(2,1)S(1)} %copy-done), kind=kOutput, calls=%fused_computation.15 | convolution fusion | flops 604766208 | bytes 3145728 | tf_op jit(solution)/shard_map/dot_general | solution.py:121
  94.1 4.9 %copy.105 = bf16[2,256,1536]{1,0,2:T(2,128)(2,1)} copy(bf16[2,256,1536]{2,1,0:T(8,128)(2,1)} %convolution_convert_fusion.1) | data formatting | bytes 3145728
  99.0 3.0 %copy.111 = bf16[192,8,2,256]{3,1,2,0:T(8,128)(2,1)} copy(bf16[192,8,2,256]{3,2,1,0:T(2,128)(2,1)} %bitcast.85) | data formatting | bytes 3145728
  102.0 2.9 %copy.97 = bf16[2,256,2,384]{3,2,0,1:T(2,128)(2,1)} copy(bf16[2,256,2,384]{1,0,3,2:T(2,128)(2,1)S(1)} %slice-done) | data formatting | bytes 1572864 | tf_op jit(solution)/shard_map/stack | solution.py:80
  104.9 3.6 %all-to-all-start.1 = ((bf16[2,256,2,384]{3,2,0,1:T(2,128)(2,1)}), bf16[2,256,2,384]{3,2,0,1:T(2,128)(2,1)S(1)}, u32[]{:S(2)}, u32[]{:S(2)}) async-start(bf16[2,256,2,384]{3,2,0,1:T(2,128)(2,1)} %copy.97), calls=%async_computation.1 | async-start | bytes 1572864 | tf_op jit(solution)/shard_map/all_to_all | solution.py:81
  111.3 27.1 %reduce-scatter.4.cloned.1.call-done = bf16[384,512]{1,0:T(8,128)(2,1)} async-done(((bf16[1536,512]{1,0:T(8,128)(2,1)}), bf16[384,512]{1,0:T(8,128)(2,1)}) %reduce-scatter.4.cloned.1.call-update) | async-done | bytes 393232
  145.8 18.0 %all_gather.3 = bf16[2,128,1536]{2,1,0:T(8,128)(2,1)S(1)} all-gather(bf16[2,128,384]{2,1,0:T(8,128)(2,1)S(1)} %dynamic-slice_select_fusion), channel_id=1, replica_groups=mesh['section'=2,'head'=4,'blk'=4] {'head'}, dimensions={2}, use_global_device_ids=true | all-gather | bytes 983040 | tf_op jit(solution)/shard_map/all_gather | solution.py:142
  (97 shorter events, 30.0 us)
Async XLA Ops:
  7.2 84.8 %copy-start = (bf16[1,384,1536]{2,1,0:T(8,128)(2,1)S(1)}, bf16[1,384,1536]{2,1,0:T(8,128)(2,1)}, u32[]{:S(2)}) copy-start(bf16[1,384,1536]{2,1,0:T(8,128)(2,1)} %param.16) | copy-start | bytes 3538948
  7.2 5.5 %copy-start.18 = (s32[4,4]{1,0:T(4,128)S(1)}, s32[4,4]{1,0:T(4,128)}, u32[]{:S(2)}) copy-start(s32[4,4]{1,0:T(4,128)} %param.20) | copy-start | bytes 196
  7.2 6.2 %copy-start.17 = (bf16[1,2,2,1536]{3,2,1,0:T(2,128)(2,1)S(1)}, bf16[1,2,2,1536]{3,2,1,0:T(2,128)(2,1)}, u32[]{:S(2)}) copy-start(bf16[1,2,2,1536]{3,2,1,0:T(2,128)(2,1)} %param.13) | copy-start | bytes 36868
  7.2 6.3 %copy-start.3 = (bf16[1,2,256,1536]{3,2,1,0:T(8,128)(2,1)S(1)}, bf16[1,2,256,1536]{3,2,1,0:T(8,128)(2,1)}, u32[]{:S(2)}) copy-start(bf16[1,2,256,1536]{3,2,1,0:T(8,128)(2,1)} %param.12) | copy-start | bytes 4718596
  7.2 42.6 %all-to-all-start = ((bf16[8,64,4,2,384]{4,3,2,1,0:T(2,128)(2,1)}), bf16[8,64,4,2,384]{4,3,2,1,0:T(2,128)(2,1)}, u32[]{:S(2)}, u32[]{:S(2)}) async-start(bf16[8,64,4,2,384]{4,3,2,1,0:T(2,128)(2,1)} %bitcast.90), calls=%async_computation | async-start | bytes 6291456 | tf_op jit(solution)/shard_map/all_to_all | solution.py:84
  12.6 125.8 %reduce-scatter.4.cloned.1.call-start = ((), (), s32[]{:S(2)}) async-start(), calls=%async_computation.3 | async-start | bytes 1966080
  32.4 3.0 %copy-start.7 = (bf16[1,2,154,2,384]{4,3,2,1,0:T(2,128)(2,1)S(1)}, bf16[1,2,154,2,384]{4,3,2,1,0:T(2,128)(2,1)}, u32[]{:S(2)}) copy-start(bf16[1,2,154,2,384]{4,3,2,1,0:T(2,128)(2,1)} %param.18) | copy-start | bytes 1419268
  34.5 7.3 %copy-start.19 = (s32[2]{0:T(128)S(1)}, s32[2]{0:T(128)}, u32[]{:S(2)}) copy-start(s32[2]{0:T(128)} %param.19) | copy-start | bytes 28
  39.7 5.6 %copy-start.8 = (bf16[2,256,1,384]{1,3,0,2:T(8,128)(2,1)S(1)}, bf16[2,256,1,384]{1,3,0,2:T(8,128)(2,1)}, u32[]{:S(2)}) copy-start(bf16[2,256,1,384]{1,3,0,2:T(8,128)(2,1)} %copy.89) | copy-start | bytes 1179652
  62.0 4.5 %copy-start.12 = (f32[2,6,256]{2,1,0:T(8,128)S(1)}, f32[2,6,256]{2,1,0:T(8,128)}, u32[]{:S(2)}) copy-start(f32[2,6,256]{2,1,0:T(8,128)} %get-tuple-element.25) | copy-start | bytes 36868
  62.0 4.5 %copy-start.13 = (f32[2,6,256]{2,1,0:T(8,128)S(1)}, f32[2,6,256]{2,1,0:T(8,128)}, u32[]{:S(2)}) copy-start(f32[2,6,256]{2,1,0:T(8,128)} %get-tuple-element.27) | copy-start | bytes 36868
  66.5 5.3 %copy-start.1 = (f32[2,6,256,1024]{3,2,1,0:T(8,128)}, f32[2,6,256,1024]{3,2,1,0:T(8,128)S(1)}, u32[]{:S(2)}) copy-start(f32[2,6,256,1024]{3,2,1,0:T(8,128)S(1)} %get-tuple-element.24) | copy-start | bytes 37748740
  66.5 5.3 %copy-start.4 = (f32[2,6,256,256]{2,3,1,0:T(8,128)S(1)}, f32[2,6,256,256]{2,3,1,0:T(8,128)}, u32[]{:S(2)}) copy-start(f32[2,6,256,256]{2,3,1,0:T(8,128)} %get-tuple-element.28) | copy-start | bytes 9437188
  73.8 6.2 %copy-start.10 = (bf16[2,256,1,384]{1,3,0,2:T(8,128)(2,1)S(1)}, bf16[2,256,1,384]{1,3,0,2:T(8,128)(2,1)}, u32[]{:S(2)}) copy-start(bf16[2,256,1,384]{1,3,0,2:T(8,128)(2,1)} %copy.93) | copy-start | bytes 1179652
  80.0 5.5 %copy-start.2 = (f32[2,6,256,1024]{3,2,1,0:T(8,128)S(1)}, f32[2,6,256,1024]{3,2,1,0:T(8,128)}, u32[]{:S(2)}) copy-start(f32[2,6,256,1024]{3,2,1,0:T(8,128)} %copy-done.1) | copy-start | bytes 37748740
  85.5 5.7 %copy-start.6 = (f32[2,6,256,154]{2,3,1,0:T(8,128)S(1)}, f32[2,6,256,154]{2,3,1,0:T(8,128)}, u32[]{:S(2)}) copy-start(f32[2,6,256,154]{2,3,1,0:T(8,128)} %get-tuple-element.26) | copy-start | bytes 5677060
  85.5 5.7 %copy-start.9 = (bf16[2,154,1,384]{1,3,0,2:T(8,128)(2,1)S(1)}, bf16[2,154,1,384]{1,3,0,2:T(8,128)(2,1)}, u32[]{:S(2)}) copy-start(bf16[2,154,1,384]{1,3,0,2:T(8,128)(2,1)} %copy.92) | copy-start | bytes 709636
  99.0 3.0 %slice-start = ((bf16[2,256,3,384]{1,0,3,2:T(2,128)(2,1)}), bf16[2,256,2,384]{1,0,3,2:T(2,128)(2,1)S(1)}, s32[]{:S(2)}) async-start(bf16[2,256,3,384]{1,0,3,2:T(2,128)(2,1)} %reshape.237), calls=%async_computation.4 | async-start | bytes 1572864 | tf_op jit(solution)/shard_map/stack | solution.py:80
  104.9 5.7 %copy-start.15 = (bf16[2,2,1536]{2,1,0:T(2,128)(2,1)S(1)}, bf16[2,2,1536]{2,1,0:T(2,128)(2,1)}, u32[]{:S(2)}) copy-start(bf16[2,2,1536]{2,1,0:T(2,128)(2,1)} %param.21) | copy-start | bytes 36868
  104.9 37.9 %all-to-all-start.1 = ((bf16[2,256,2,384]{3,2,0,1:T(2,128)(2,1)}), bf16[2,256,2,384]{3,2,0,1:T(2,128)(2,1)S(1)}, u32[]{:S(2)}, u32[]{:S(2)}) async-start(bf16[2,256,2,384]{3,2,0,1:T(2,128)(2,1)} %copy.97), calls=%async_computation.1 | async-start | bytes 1572864 | tf_op jit(solution)/shard_map/all_to_all | solution.py:81
  142.2 2.5 %collective-permute-start = (bf16[2,256,384]{2,1,0:T(8,128)(2,1)}, bf16[2,256,384]{2,1,0:T(8,128)(2,1)}, u32[]{:S(2)}, u32[]{:S(2)}) collective-permute-start(bf16[2,256,384]{2,1,0:T(8,128)(2,1)} %fusion.28), channel_id=1, source_target_pairs={{0,16},{16,0},{1,17},{17,1},{2,18},{18,2},{3,19},{19,3},{4,20},{20... | collective-permute-start | bytes 1179656 | tf_op jit(solution)/shard_map/ppermute | solution.py:14
  142.9 21.5 %copy-start.14 = (f32[2,1536]{1,0:T(2,128)S(1)}, f32[2,1536]{1,0:T(2,128)}, u32[]{:S(2)}) copy-start(f32[2,1536]{1,0:T(2,128)} %get-tuple-element.32) | copy-start | bytes 36868
  143.0 21.7 %copy-start.11 = (bf16[1536,64]{0,1:T(8,128)(2,1)S(1)}, bf16[1536,64]{0,1:T(8,128)(2,1)}, u32[]{:S(2)}) copy-start(bf16[1536,64]{0,1:T(8,128)(2,1)} %param.22) | copy-start | bytes 589828
  144.7 20.6 %copy-start.16 = (f32[1,64,128]{2,1,0:T(8,128)S(1)}, f32[1,64,128]{2,1,0:T(8,128)}, u32[]{:S(2)}) copy-start(f32[1,64,128]{2,1,0:T(8,128)} %param.23) | copy-start | bytes 98308
  (1 other events, 1.5 us)
Sparse Core Ops, SparseCore 0:
  102.1 36.2 reduce-scatter.3
where the time goes:
time: 176 us; the launch traced here: 175 us
  local copies, waits for them, and re-layouts  63.3 us (36%)
  waiting for transfers between devices  28.7 us (16%)
  matrix products  27.7 us (16%)
  blocking collectives  18 us (10%)
  between operations  14.4 us (8%)
  other arithmetic  13.4 us (8%)
  starting transfers between devices  9.07 us (5%)
    unnamed x2, waiting for transfers between devices  27.1 us
    unnamed x49, local copies, waits for them, and re-layouts  25.6 us
    all_gather x1, blocking collectives, shards(): final_rows = lax.all_gather(last_half, 'head', axis=2, tiled=True)  18 us
    dot_general x3, matrix products, piece_scores(): jnp.einsum('sqhd,skhd->shqk', query_heads, key_heads, preferred_element_t...  10.8 us
    dot_general x3, matrix products, piece_values(): jnp.einsum('shqk,skhd->sqhd', probs_piece, value_heads, preferred_element...  9.17 us
    another operation x1, local copies, waits for them, and re-layouts, piece_values(): value_heads = value_piece.reshape(seq_dev, -1, head_count, HEAD_DIM)  6.13 us
    another operation x1, local copies, waits for them, and re-layouts, piece_scores(): key_heads = key_piece.reshape(seq_dev, -1, head_count, HEAD_DIM)  6.03 us
    all_to_all x1, starting transfers between devices, shards(): lax.all_to_all(local_cache, 'blk', split_axis=0, concat_axis=1, tiled=True)  5.44 us
  transfers between devices with their start and end apart: 4, of which 2 were waited for; matrix products, arithmetic and copies ran while one was open for 27% of the time, Pallas kernels for 0%

commit v1 on v0

--- a/solution.py
+++ b/solution.py
@@ -139,7 +139,15 @@
     received = passed_along(layer_out, "section", 1)
     last_layer = jnp.where(section_index == 0, received, layer_out)
     last_half = lax.dynamic_slice_in_dim(last_layer, section_index * half_rows, half_rows, 1)
-    final_rows = lax.all_gather(last_half, "head", axis=2, tiled=True)
+    ways, here = (lax.axis_size("head"), lax.axis_index("head"))
+    grown, reach = (last_half, 1)
+    while reach < ways:
+        theirs = lax.ppermute(grown, "head", [(d, d ^ reach) for d in range(ways)])
+        mine_first = jnp.concatenate([grown, theirs], axis=2)
+        theirs_first = jnp.concatenate([theirs, grown], axis=2)
+        grown = jnp.where(here & reach == 0, mine_first, theirs_first)
+        reach = 2 * reach
+    final_rows = grown
     final_shift = final_mod.astype(jnp.float32)
     final_normed = (
         layer_norm(final_rows.astype(jnp.float32)) * (1.0 + final_shift[:, 1:2])

time: 176 us -> 188 us (1.068)
  waiting for transfers between devices: 28.7 us -> 55.9 us
  blocking collectives: 18 us -> 0 us
  starting transfers between devices: 9.07 us -> 11 us
    ppermute x0 -> x2, waiting for transfers between devices: none -> 20.1 us  [shards(): theirs = lax.ppermute(grown, 'head', [(d, d ^ reach) for d in range(ways)])]
    all_gather x1 -> x0, blocking collectives: 18 us -> none  [shards(): final_rows = lax.all_gather(last_half, 'head', axis=2, tiled=True)]
    unnamed x2, waiting for transfers between devices: 27.1 us -> 33.8 us
    ppermute x0 -> x2, starting transfers between devices: none -> 1.92 us  [shards(): theirs = lax.ppermute(grown, 'head', [(d, d ^ reach) for d in range(ways)])]
  transfers between devices with their start and end apart: 4 -> 6, of which waited for: 2 -> 5; matrix products, arithmetic and copies ran while one was open for 27% -> 25% of each run, Pallas kernels for 0% -> 0%
where the time goes in v1:
time: 188 us; the launch traced here: 187 us
  local copies, waits for them, and re-layouts  63.5 us (34%)
  waiting for transfers between devices  55.9 us (30%)
  matrix products  27.7 us (15%)
  between operations  14.4 us (8%)
  other arithmetic  14.1 us (8%)
  starting transfers between devices  11 us (6%)
    unnamed x2, waiting for transfers between devices  33.8 us
    unnamed x49, local copies, waits for them, and re-layouts  25.2 us
    ppermute x2, waiting for transfers between devices, shards(): theirs = lax.ppermute(grown, 'head', [(d, d ^ reach) for d in range(ways)])  20.1 us
    dot_general x3, matrix products, piece_scores(): jnp.einsum('sqhd,skhd->shqk', query_heads, key_heads, preferred_element_t...  10.8 us
    dot_general x3, matrix products, piece_values(): jnp.einsum('shqk,skhd->sqhd', probs_piece, value_heads, preferred_element...  9.17 us
    another operation x1, local copies, waits for them, and re-layouts, piece_values(): value_heads = value_piece.reshape(seq_dev, -1, head_count, HEAD_DIM)  6.16 us
    another operation x1, local copies, waits for them, and re-layouts, piece_scores(): key_heads = key_piece.reshape(seq_dev, -1, head_count, HEAD_DIM)  6.02 us
    all_to_all x1, starting transfers between devices, shards(): lax.all_to_all(local_cache, 'blk', split_axis=0, concat_axis=1, tiled=True)  5.44 us
  transfers between devices with their start and end apart: 6, of which 5 were waited for; matrix products, arithmetic and copies ran while one was open for 25% of the time, Pallas kernels for 0%

profile of v1, /device:TPU:0, one launch (start us, length us, event | category | flops | bytes accessed | tf_op | source)
XLA Modules:
  0.0 186.7 jit_solution(8921055538020342067)
XLA Ops:
  7.2 5.4 %all-to-all-start = ((bf16[8,64,4,2,384]{4,3,2,1,0:T(2,128)(2,1)}), bf16[8,64,4,2,384]{4,3,2,1,0:T(2,128)(2,1)}, u32[]{:S(2)}, u32[]{:S(2)}) async-start(bf16[8,64,4,2,384]{4,3,2,1,0:T(2,128)(2,1)} %bitcast.105), calls=%async_computation | async-start | bytes 6291456 | tf_op jit(solution)/shard_map/all_to_all | solution.py:84
  14.3 6.1 %copy.85 = bf16[1,1536,3,384]{1,3,2,0:T(8,128)(2,1)} copy(bf16[1,1536,3,384]{3,1,2,0:T(8,128)(2,1)} %param.15) | data formatting | bytes 7077888 | tf_op args[3]
  21.1 5.2 %convolution_convert_fusion = bf16[512,1152]{1,0:T(8,128)(2,1)} fusion(bf16[512,1536]{1,0:T(8,128)(2,1)S(1)} %bitcast.110, bf16[1536,1152]{0,1:T(8,128)(2,1)} %bitcast.103), kind=kOutput, calls=%fused_computation.14 | convolution fusion | flops 1812529152 | bytes 6291456 | tf_op jit(solution)/shard_map/dot_general | solution.py:71
  26.3 2.4 %copy.86 = bf16[512,1152]{0,1:T(8,128)(2,1)} copy(bf16[512,1152]{1,0:T(8,128)(2,1)} %convolution_convert_fusion) | data formatting | bytes 2359296 | tf_op jit(solution)/shard_map/convert_element_type | solution.py:75
  28.7 3.7 %reshape.258 = bf16[2,256,3,384]{1,0,3,2:T(2,128)(2,1)} reshape(bf16[512,1152]{0,1:T(8,128)(2,1)} %copy.86) | data formatting | bytes 2359296 | tf_op jit(solution)/shard_map/reshape | solution.py:76
  41.9 3.5 %fusion.7 = (f32[2,6,256]{2,1,0:T(8,128)}, f32[2,6,256,154]{2,3,1,0:T(8,128)}) fusion(pred[2,154]{1,0:T(4,128)(4,1)S(1)} %iota_compare_fusion, bf16[2,256,6,64]{1,3,2,0:T(8,128)(2,1)S(1)} %bitcast.100, bf16[2,154,6,64]{1,3,2,0:T(8,128)(2,1)} %bitcast.111), kind=kOutput, calls=%fused_computation.24 | convolution fusion | flops 61971456 | bytes 2534708 | tf_op jit(solution)/shard_map/sqhd,skhd->shqk/dot_general | solution.py:28
  45.3 2.9 %multiply_reduce_fusion.1 = (f32[2,6,256]{2,1,0:T(8,128)}, f32[2,6,256,256]{2,3,1,0:T(8,128)}) fusion(bf16[2,256,6,64]{1,3,2,0:T(8,128)(2,1)S(1)} %bitcast.101, bf16[2,256,6,64]{1,3,2,0:T(8,128)(2,1)S(1)} %bitcast.113), kind=kOutput, calls=%fused_computation.16 | convolution fusion | flops 102233088 | bytes 3944448 | tf_op jit(solution)/shard_map/sqhd,skhd->shqk/dot_general | solution.py:28
  49.8 3.4 %copy.90 = bf16[2,4,64,4,2,384]{5,3,2,1,0,4:T(4,128)(2,1)S(1)} copy(bf16[2,4,64,4,2,384]{5,4,3,2,0,1:T(2,128)(2,1)} %bitcast.13) | data formatting | bytes 6291456 | tf_op jit(solution)/shard_map/all_to_all | solution.py:84
  53.2 2.8 %fusion.32 = (bf16[2,256,4,1,384]{4,2,1,0,3:T(4,128)(2,1)}, bf16[2,256,4,1,384]{4,2,1,0,3:T(4,128)(2,1)}) fusion(bf16[2,256,4,2,384]{4,2,1,0,3:T(4,128)(2,1)S(1)} %bitcast.97), kind=kLoop, calls=%fused_computation.74 | loop fusion | bytes 6291456 | tf_op jit(solution)/shard_map/slice | solution.py:87
  56.0 6.0 %reshape_reshape_squeeze.6 = bf16[2,1024,6,64]{3,2,1,0:T(8,128)(2,1)} reshape(bf16[2,256,4,1,384]{4,2,1,0,3:T(4,128)(2,1)} %get-tuple-element.12) | data formatting | bytes 3145728 | tf_op jit(solution)/shard_map/reshape;reshape;squeeze | solution.py:27
  62.1 4.4 %fusion = (f32[2,6,256]{2,1,0:T(8,128)S(1)}, f32[2,6,256,1024]{3,2,1,0:T(8,128)S(1)}) fusion(pred[2,1024]{1,0:T(4,128)(4,1)S(1)} %tile.9, bf16[2,256,6,64]{1,3,2,0:T(8,128)(2,1)S(1)} %bitcast.102, bf16[2,1024,6,64]{3,2,1,0:T(8,128)(2,1)} %reshape_reshape_squeeze.6), kind=kOutput, calls=%fused_computation.3 | convolution fusion | flops 412087296 | bytes 14563328 | tf_op jit(solution)/shard_map/sqhd,skhd->shqk/dot_general | solution.py:28
  66.6 3.3 %fusion.1 = f32[2,6,256]{2,1,0:T(8,128)S(1)} fusion(f32[2,6,256,1024]{3,2,1,0:T(8,128)S(1)} %get-tuple-element.26, f32[2,6,256]{2,1,0:T(8,128)S(1)} %maximum_maximum_fusion, pred[2,1024]{1,0:T(4,128)(4,1)S(1)} %tile.9), kind=kLoop, calls=%fused_computation.4 | loop fusion | flops 12579840 | bytes 12609536 | tf_op jit(solution)/shard_map/reduce_sum | solution.py:110
  73.9 6.2 %reshape_reshape_squeeze.7 = bf16[2,1024,6,64]{3,2,1,0:T(8,128)(2,1)} reshape(bf16[2,256,4,1,384]{4,2,1,0,3:T(4,128)(2,1)} %get-tuple-element.13) | data formatting | bytes 3145728 | tf_op jit(solution)/shard_map/reshape;reshape;squeeze | solution.py:38
  80.0 2.8 %fusion.13 = f32[2,256,6,64]{1,3,2,0:T(8,128)S(1)} fusion(bf16[2,256,6,64]{1,3,2,0:T(8,128)(2,1)S(1)} %bitcast.118, f32[2,6,256,256]{2,3,1,0:T(8,128)} %get-tuple-element.30, f32[2,6,256]{2,1,0:T(8,128)S(1)} %add_add_fusion, f32[2,6,256]{2,1,0:T(8,128)S(1)} %maximum_maximum_fusion), kind=kOutput, calls=%fused_computation.32 | convolution fusion | flops 103809024 | bytes 4349952 | tf_op jit(solution)/shard_map/shqk,skhd->sqhd/dot_general | solution.py:39
  82.9 2.7 %copy-done.2 = f32[2,6,256,1024]{3,2,1,0:T(8,128)S(1)} copy-done((f32[2,6,256,1024]{3,2,1,0:T(8,128)S(1)}, f32[2,6,256,1024]{3,2,1,0:T(8,128)}, u32[]{:S(2)}) %copy-start.2) | copy-done | bytes 12582936
  85.6 5.7 %fusion.16 = f32[2,256,6,64]{1,3,2,0:T(8,128)S(1)} fusion(bf16[2,1024,6,64]{3,2,1,0:T(8,128)(2,1)} %reshape_reshape_squeeze.7, f32[2,6,256,1024]{3,2,1,0:T(8,128)S(1)} %copy-done.2, f32[2,6,256]{2,1,0:T(8,128)S(1)} %add_add_fusion, f32[2,6,256]{2,1,0:T(8,128)S(1)} %maximum_maximum_fusion, pred[2,1024]{1,0:T(4,128)(4,1)S(1)} %tile.9), kind=kOutput, calls=%fused_computation.36 | convolution fusion | flops 418381824 | bytes 14968832 | tf_op jit(solution)/shard_map/shqk,skhd->sqhd/dot_general | solution.py:39
  92.0 2.2 %convolution_convert_fusion.1 = bf16[2,256,1536]{2,1,0:T(8,128)(2,1)} fusion(bf16[2,256,384]{1,2,0:T(8,128)(2,1)S(1)} %bitcast.116, bf16[1,384,1536]{2,1,0:T(8,128)(2,1)S(1)} %copy-done), kind=kOutput, calls=%fused_computation.15 | convolution fusion | flops 604766208 | bytes 3145728 | tf_op jit(solution)/shard_map/dot_general | solution.py:121
  94.1 4.9 %copy.105 = bf16[2,256,1536]{1,0,2:T(2,128)(2,1)} copy(bf16[2,256,1536]{2,1,0:T(8,128)(2,1)} %convolution_convert_fusion.1) | data formatting | bytes 3145728
  99.0 2.9 %copy.111 = bf16[192,8,2,256]{3,1,2,0:T(8,128)(2,1)} copy(bf16[192,8,2,256]{3,2,1,0:T(2,128)(2,1)} %bitcast.99) | data formatting | bytes 3145728
  104.7 33.7 %reduce-scatter.4.cloned.1.call-done = bf16[384,512]{1,0:T(8,128)(2,1)} async-done(((bf16[1536,512]{1,0:T(8,128)(2,1)}), bf16[384,512]{1,0:T(8,128)(2,1)}) %reduce-scatter.4.cloned.1.call-update) | async-done | bytes 393232
  142.2 2.9 %copy.97 = bf16[2,256,2,384]{3,2,0,1:T(2,128)(2,1)} copy(bf16[2,256,2,384]{1,0,3,2:T(2,128)(2,1)S(1)} %slice-done) | data formatting | bytes 1572864 | tf_op jit(solution)/shard_map/stack | solution.py:80
  145.1 3.7 %all-to-all-start.1 = ((bf16[2,256,2,384]{3,2,0,1:T(2,128)(2,1)}), bf16[2,256,2,384]{3,2,0,1:T(2,128)(2,1)S(1)}, u32[]{:S(2)}, u32[]{:S(2)}) async-start(bf16[2,256,2,384]{3,2,0,1:T(2,128)(2,1)} %copy.97), calls=%async_computation.1 | async-start | bytes 1572864 | tf_op jit(solution)/shard_map/all_to_all | solution.py:81
  151.4 5.5 %collective-permute-done.1 = bf16[2,128,384]{2,1,0:T(8,128)(2,1)S(1)} collective-permute-done((bf16[2,128,384]{2,1,0:T(8,128)(2,1)S(1)}, bf16[2,128,384]{2,1,0:T(8,128)(2,1)S(1)}, u32[]{:S(2)}, u32[]{:S(2)}) %collective-permute-start.1) | collective-permute-done | bytes 196640 | tf_op jit(solution)/shard_map/ppermute | solution.py:145
  162.3 14.6 %collective-permute-done.2 = bf16[2,128,768]{2,1,0:T(8,128)(2,1)S(1)} collective-permute-done((bf16[2,128,768]{2,1,0:T(8,128)(2,1)S(1)}, bf16[2,128,768]{2,1,0:T(8,128)(2,1)S(1)}, u32[]{:S(2)}, u32[]{:S(2)}) %collective-permute-start.2) | collective-permute-done | bytes 393248 | tf_op jit(solution)/shard_map/ppermute | solution.py:145
  (102 shorter events, 35.4 us)
Async XLA Ops:
  7.2 84.8 %copy-start = (bf16[1,384,1536]{2,1,0:T(8,128)(2,1)S(1)}, bf16[1,384,1536]{2,1,0:T(8,128)(2,1)}, u32[]{:S(2)}) copy-start(bf16[1,384,1536]{2,1,0:T(8,128)(2,1)} %param.16) | copy-start | bytes 3538948
  7.2 5.5 %copy-start.18 = (s32[4,4]{1,0:T(4,128)S(1)}, s32[4,4]{1,0:T(4,128)}, u32[]{:S(2)}) copy-start(s32[4,4]{1,0:T(4,128)} %param.20) | copy-start | bytes 196
  7.2 6.2 %copy-start.17 = (bf16[1,2,2,1536]{3,2,1,0:T(2,128)(2,1)S(1)}, bf16[1,2,2,1536]{3,2,1,0:T(2,128)(2,1)}, u32[]{:S(2)}) copy-start(bf16[1,2,2,1536]{3,2,1,0:T(2,128)(2,1)} %param.13) | copy-start | bytes 36868
  7.2 6.3 %copy-start.3 = (bf16[1,2,256,1536]{3,2,1,0:T(8,128)(2,1)S(1)}, bf16[1,2,256,1536]{3,2,1,0:T(8,128)(2,1)}, u32[]{:S(2)}) copy-start(bf16[1,2,256,1536]{3,2,1,0:T(8,128)(2,1)} %param.12) | copy-start | bytes 4718596
  7.2 42.6 %all-to-all-start = ((bf16[8,64,4,2,384]{4,3,2,1,0:T(2,128)(2,1)}), bf16[8,64,4,2,384]{4,3,2,1,0:T(2,128)(2,1)}, u32[]{:S(2)}, u32[]{:S(2)}) async-start(bf16[8,64,4,2,384]{4,3,2,1,0:T(2,128)(2,1)} %bitcast.105), calls=%async_computation | async-start | bytes 6291456 | tf_op jit(solution)/shard_map/all_to_all | solution.py:84
  12.6 125.8 %reduce-scatter.4.cloned.1.call-start = ((), (), s32[]{:S(2)}) async-start(), calls=%async_computation.3 | async-start | bytes 1966080
  35.3 6.4 %copy-start.19 = (s32[2]{0:T(128)S(1)}, s32[2]{0:T(128)}, u32[]{:S(2)}) copy-start(s32[2]{0:T(128)} %param.19) | copy-start | bytes 28
  39.7 5.6 %copy-start.8 = (bf16[2,256,1,384]{1,3,0,2:T(8,128)(2,1)S(1)}, bf16[2,256,1,384]{1,3,0,2:T(8,128)(2,1)}, u32[]{:S(2)}) copy-start(bf16[2,256,1,384]{1,3,0,2:T(8,128)(2,1)} %copy.89) | copy-start | bytes 1179652
  62.1 4.5 %copy-start.13 = (f32[2,6,256]{2,1,0:T(8,128)S(1)}, f32[2,6,256]{2,1,0:T(8,128)}, u32[]{:S(2)}) copy-start(f32[2,6,256]{2,1,0:T(8,128)} %get-tuple-element.29) | copy-start | bytes 36868
  66.5 5.3 %copy-start.1 = (f32[2,6,256,1024]{3,2,1,0:T(8,128)}, f32[2,6,256,1024]{3,2,1,0:T(8,128)S(1)}, u32[]{:S(2)}) copy-start(f32[2,6,256,1024]{3,2,1,0:T(8,128)S(1)} %get-tuple-element.26) | copy-start | bytes 37748740
  66.5 5.3 %copy-start.4 = (f32[2,6,256,256]{2,3,1,0:T(8,128)S(1)}, f32[2,6,256,256]{2,3,1,0:T(8,128)}, u32[]{:S(2)}) copy-start(f32[2,6,256,256]{2,3,1,0:T(8,128)} %get-tuple-element.30) | copy-start | bytes 9437188
  73.9 6.2 %copy-start.10 = (bf16[2,256,1,384]{1,3,0,2:T(8,128)(2,1)S(1)}, bf16[2,256,1,384]{1,3,0,2:T(8,128)(2,1)}, u32[]{:S(2)}) copy-start(bf16[2,256,1,384]{1,3,0,2:T(8,128)(2,1)} %copy.93) | copy-start | bytes 1179652
  80.0 5.5 %copy-start.2 = (f32[2,6,256,1024]{3,2,1,0:T(8,128)S(1)}, f32[2,6,256,1024]{3,2,1,0:T(8,128)}, u32[]{:S(2)}) copy-start(f32[2,6,256,1024]{3,2,1,0:T(8,128)} %copy-done.1) | copy-start | bytes 37748740
  85.6 5.7 %copy-start.6 = (f32[2,6,256,154]{2,3,1,0:T(8,128)S(1)}, f32[2,6,256,154]{2,3,1,0:T(8,128)}, u32[]{:S(2)}) copy-start(f32[2,6,256,154]{2,3,1,0:T(8,128)} %get-tuple-element.28) | copy-start | bytes 5677060
  85.6 5.7 %copy-start.9 = (bf16[2,154,1,384]{1,3,0,2:T(8,128)(2,1)S(1)}, bf16[2,154,1,384]{1,3,0,2:T(8,128)(2,1)}, u32[]{:S(2)}) copy-start(bf16[2,154,1,384]{1,3,0,2:T(8,128)(2,1)} %copy.92) | copy-start | bytes 709636
  104.7 37.5 %slice-start = ((bf16[2,256,3,384]{1,0,3,2:T(2,128)(2,1)}), bf16[2,256,2,384]{1,0,3,2:T(2,128)(2,1)S(1)}, s32[]{:S(2)}) async-start(bf16[2,256,3,384]{1,0,3,2:T(2,128)(2,1)} %reshape.258), calls=%async_computation.4 | async-start | bytes 1572864 | tf_op jit(solution)/shard_map/stack | solution.py:80
  142.2 6.6 %copy-start.15 = (bf16[2,2,1536]{2,1,0:T(2,128)(2,1)S(1)}, bf16[2,2,1536]{2,1,0:T(2,128)(2,1)}, u32[]{:S(2)}) copy-start(bf16[2,2,1536]{2,1,0:T(2,128)(2,1)} %param.21) | copy-start | bytes 36868
  142.2 6.6 %collective-permute-start = (bf16[2,256,384]{2,1,0:T(8,128)(2,1)}, bf16[2,256,384]{2,1,0:T(8,128)(2,1)S(1)}, u32[]{:S(2)}, u32[]{:S(2)}) collective-permute-start(bf16[2,256,384]{2,1,0:T(8,128)(2,1)} %fusion.25), channel_id=1, source_target_pairs={{0,16},{16,0},{1,17},{17,1},{2,18},{18,2},{3,19},{19,3},{4,20},{20... | collective-permute-start | bytes 1179656 | tf_op jit(solution)/shard_map/ppermute | solution.py:14
  145.1 15.2 %all-to-all-start.1 = ((bf16[2,256,2,384]{3,2,0,1:T(2,128)(2,1)}), bf16[2,256,2,384]{3,2,0,1:T(2,128)(2,1)S(1)}, u32[]{:S(2)}, u32[]{:S(2)}) async-start(bf16[2,256,2,384]{3,2,0,1:T(2,128)(2,1)} %copy.97), calls=%async_computation.1 | async-start | bytes 1572864 | tf_op jit(solution)/shard_map/all_to_all | solution.py:81
  149.8 7.2 %collective-permute-start.1 = (bf16[2,128,384]{2,1,0:T(8,128)(2,1)S(1)}, bf16[2,128,384]{2,1,0:T(8,128)(2,1)S(1)}, u32[]{:S(2)}, u32[]{:S(2)}) collective-permute-start(bf16[2,128,384]{2,1,0:T(8,128)(2,1)S(1)} %dynamic-slice_select_fusion), channel_id=1, source_target_pairs={{0,4},{4,0},{8,12},{12,8},{1,5},{5,1},{9,13},{13,9},{2,6},{6,2},{1... | collective-permute-start | bytes 589832 | tf_op jit(solution)/shard_map/ppermute | solution.py:145
  157.1 19.8 %collective-permute-start.2 = (bf16[2,128,768]{2,1,0:T(8,128)(2,1)S(1)}, bf16[2,128,768]{2,1,0:T(8,128)(2,1)S(1)}, u32[]{:S(2)}, u32[]{:S(2)}) collective-permute-start(bf16[2,128,768]{2,1,0:T(8,128)(2,1)S(1)} %maximum_select_fusion.3), channel_id=1, source_target_pairs={{0,8},{4,12},{8,0},{12,4},{1,9},{5,13},{9,1},{13,5},{2,10},{6,14},... | collective-permute-start | bytes 1179656 | tf_op jit(solution)/shard_map/ppermute | solution.py:145
  160.5 17.0 %copy-start.14 = (f32[2,1536]{1,0:T(2,128)S(1)}, f32[2,1536]{1,0:T(2,128)}, u32[]{:S(2)}) copy-start(f32[2,1536]{1,0:T(2,128)} %get-tuple-element.34) | copy-start | bytes 36868
  162.2 15.7 %copy-start.11 = (bf16[1536,64]{0,1:T(8,128)(2,1)S(1)}, bf16[1536,64]{0,1:T(8,128)(2,1)}, u32[]{:S(2)}) copy-start(bf16[1536,64]{0,1:T(8,128)(2,1)} %param.22) | copy-start | bytes 589828
  162.3 16.1 %copy-start.16 = (f32[1,64,128]{2,1,0:T(8,128)S(1)}, f32[1,64,128]{2,1,0:T(8,128)}, u32[]{:S(2)}) copy-start(f32[1,64,128]{2,1,0:T(8,128)} %param.23) | copy-start | bytes 98308
  (3 other events, 8.9 us)
Sparse Core Ops, SparseCore 0:
  102.0 36.3 reduce-scatter.3
